TPU v7x, 32 devices: a whole 2x2x4 slice. The times are simulated.
32 devices in a mesh: group: 4 (over y, core), seq: 2 (over x), rep: 4 (over z).
Axes of the slice: x: 2, y: 2, z: 4, core: 2. Of those that a mesh axis runs over, the one named last changes fastest.
Arguments:
- query_raw: bfloat16 [4, 4, 256, 3072], P('rep', 'group', 'seq'), may hold values from -1000 to 1000
- key_raw: bfloat16 [4, 4, 256, 3072], P('rep', 'group', 'seq'), may hold values from -1000 to 1000
- value_in: bfloat16 [4, 4, 256, 3072], P('rep', 'group', 'seq'), may hold values from -6 to 6
- out_cotangent: bfloat16 [4, 4, 256, 3072], P('rep', 'group', 'seq'), may hold values from -25 to 25
- query_gain: float32 [3072], replicated, may hold values from 0.5 to 1.5
- key_gain: float32 [3072], replicated, may hold values from 0.5 to 1.5
- attend_from: int32 [4, 4], P('rep', 'group'), may hold values from 0 to 3, as said below
Outputs:
- query_grad: bfloat16 [4, 4, 256, 3072], P('rep', 'group', 'seq')
- key_grad: bfloat16 [4, 4, 256, 3072], P('rep', 'group', 'seq')
- value_grad: bfloat16 [4, 4, 256, 3072], P('rep', 'group', 'seq')
- query_gain_grad: float32 [3072], P('rep')
- key_gain_grad: float32 [3072], P('rep')
Inputs may be any that keep to these rules, and one draw needn't show every extreme that they name: For group c, max(0, c - 2) <= attend_from[b, c] <= c.
All inputs are finite; a program needn't handle non-finite values.
Results may differ from a plain program's by a relative error of at most 0.012.
The roundings to bfloat16 on the way count: a program that leaves them out, or rounds other values in their place, can miss the bound.
Values may be sent and summed in bfloat16 or wider, within the bound.
A program may use at most 128 MiB of HBM per device.

v0:
```python
import jax
import jax.numpy as jnp
from jax import lax
from jax.sharding import PartitionSpec as P

HEAD_DIM = 128
PAST = 2


EPSILON = 1e-06


def from_behind(block, axis, distance):
    devices = range(lax.axis_size(axis))
    route = [(i - distance, i) for i in devices if i - distance in devices]
    return lax.ppermute(block, axis, route)


def normalize(row_values, gain_vec):
    values = row_values.astype(jnp.float32)
    inv_rms = lax.rsqrt(jnp.mean(values * values, axis=-1, keepdims=True) + EPSILON)
    return (values, inv_rms, (values * inv_rms * gain_vec).astype(jnp.bfloat16))


def denormalize(values, inv_rms, gain_vec, grad_low):
    upstream = grad_low.astype(jnp.float32)
    weighted = upstream * gain_vec
    inner_mean = jnp.mean(values * weighted, axis=-1, keepdims=True)
    result = inv_rms * weighted - values * (inv_rms * inv_rms * inv_rms) * inner_mean
    gain_terms = jnp.sum(upstream * values * inv_rms, axis=0)
    return (result.astype(jnp.bfloat16), gain_terms)


def head_pass(query_head, key_head, value_head, cot_head, visible, factor):
    scores = jnp.dot(query_head, key_head.T, preferred_element_type=jnp.float32) * factor
    scores = jnp.where(visible[None, :], scores, -1e30)
    row_max = jnp.max(scores, axis=1, keepdims=True)
    weights = jnp.exp(scores - row_max)
    row_total = jnp.sum(weights, axis=1, keepdims=True)
    probabilities = weights / row_total
    probs_low = probabilities.astype(jnp.bfloat16)
    dprobs = jnp.dot(cot_head, value_head.T, preferred_element_type=jnp.float32)
    row_delta = jnp.sum(probabilities * dprobs, axis=1, keepdims=True)
    dscores = (probabilities * (dprobs - row_delta)).astype(jnp.bfloat16)
    query_part = jnp.dot(dscores, key_head, preferred_element_type=jnp.float32) * factor
    key_part = jnp.dot(dscores.T, query_head, preferred_element_type=jnp.float32) * factor
    value_part = jnp.dot(probs_low.T, cot_head, preferred_element_type=jnp.float32)
    return (query_part, key_part, value_part, row_max[:, 0], row_total[:, 0], row_delta[:, 0])


def pass_forward(kv_pair, hop_count):
    return from_behind(kv_pair, "group", hop_count)


def pass_back(cotangent_pair, hop_count):
    return from_behind(cotangent_pair, "group", hop_count)


def body(query_raw, key_raw, value_in, out_cotangent, query_gain, key_gain, attend_from):
    tok_rows = query_raw.shape[2]
    feature_width = query_raw.shape[3]
    q_values, q_inv, q_normed = normalize(query_raw.reshape(tok_rows, feature_width), query_gain)
    k_values, k_inv, k_normed = normalize(key_raw.reshape(tok_rows, feature_width), key_gain)
    heads_q, heads_k, heads_v, heads_cot = (
        lax.all_to_all(q_normed, "seq", split_axis=1, concat_axis=0, tiled=True),
        lax.all_to_all(k_normed, "seq", split_axis=1, concat_axis=0, tiled=True),
        lax.all_to_all(
            value_in.reshape(tok_rows, feature_width),
            "seq",
            split_axis=1,
            concat_axis=0,
            tiled=True,
        ),
        lax.all_to_all(
            out_cotangent.reshape(tok_rows, feature_width),
            "seq",
            split_axis=1,
            concat_axis=0,
            tiled=True,
        ),
    )
    group_len = heads_q.shape[0]
    head_width = heads_q.shape[1]
    window_len = PAST + 1
    own_pair = jnp.stack((heads_k, heads_v))
    earlier = []
    current = own_pair
    for hop_count in range(PAST):
        current = pass_forward(current, 1)
        earlier.insert(0, current)
    stacked = jnp.concatenate(earlier + [own_pair], axis=1)
    key_window = stacked[0]
    value_window = stacked[1]
    group_index = lax.axis_index("group")
    key_owner = (
        group_index - PAST + jnp.arange(window_len * group_len, dtype=jnp.int32) // group_len
    )
    visible = key_owner >= attend_from[0, 0]
    factor = HEAD_DIM ** (-0.5)
    query_block = 512 if group_len % 512 == 0 else group_len
    count_heads = head_width // HEAD_DIM
    key_rows_count = window_len * group_len

    def one_head(head_index, state_tuple):
        query_acc, key_acc, value_acc, max_acc, total_acc, delta_acc = state_tuple
        column_start = head_index * HEAD_DIM
        q_head = lax.dynamic_slice_in_dim(heads_q, column_start, HEAD_DIM, 1)
        cot_head = lax.dynamic_slice_in_dim(heads_cot, column_start, HEAD_DIM, 1)
        key_head = lax.dynamic_slice_in_dim(key_window, column_start, HEAD_DIM, 1)
        value_head = lax.dynamic_slice_in_dim(value_window, column_start, HEAD_DIM, 1)
        key_sum = jnp.zeros((key_rows_count, HEAD_DIM), jnp.float32)
        value_sum = jnp.zeros((key_rows_count, HEAD_DIM), jnp.float32)
        query_rows = []
        max_rows = []
        total_rows = []
        delta_rows = []
        for row_start in range(0, group_len, query_block):
            query_part, key_part, value_part, row_max, row_total, row_delta = head_pass(
                q_head[row_start : row_start + query_block],
                key_head,
                value_head,
                cot_head[row_start : row_start + query_block],
                visible,
                factor,
            )
            query_rows.append(query_part)
            max_rows.append(row_max)
            total_rows.append(row_total)
            delta_rows.append(row_delta)
            key_sum = key_sum + key_part
            value_sum = value_sum + value_part
        query_acc = lax.dynamic_update_slice_in_dim(
            query_acc, jnp.concatenate(query_rows, axis=0), column_start, 1
        )
        key_acc = lax.dynamic_update_slice_in_dim(key_acc, key_sum, column_start, 1)
        value_acc = lax.dynamic_update_slice_in_dim(value_acc, value_sum, column_start, 1)
        max_acc = lax.dynamic_update_slice_in_dim(
            max_acc, jnp.concatenate(max_rows)[:, None], head_index, 1
        )
        total_acc = lax.dynamic_update_slice_in_dim(
            total_acc, jnp.concatenate(total_rows)[:, None], head_index, 1
        )
        delta_acc = lax.dynamic_update_slice_in_dim(
            delta_acc, jnp.concatenate(delta_rows)[:, None], head_index, 1
        )
        return (query_acc, key_acc, value_acc, max_acc, total_acc, delta_acc)

    initial = (
        jnp.zeros((group_len, head_width), jnp.float32),
        jnp.zeros((key_rows_count, head_width), jnp.float32),
        jnp.zeros((key_rows_count, head_width), jnp.float32),
        jnp.zeros((group_len, count_heads), jnp.float32),
        jnp.zeros((group_len, count_heads), jnp.float32),
        jnp.zeros((group_len, count_heads), jnp.float32),
    )
    query_acc, key_acc, value_acc, max_all, total_all, delta_all = lax.fori_loop(
        0, count_heads, one_head, initial
    )
    cotangent_pair = jnp.stack((key_acc, value_acc))
    own_total = cotangent_pair[:, 0:group_len]
    for hop_count in range(1, PAST + 1):
        lower_row = hop_count * group_len
        own_total = pass_back(own_total, -1) + cotangent_pair[:, lower_row : lower_row + group_len]
    query_heads = query_acc.astype(jnp.bfloat16)
    key_heads = own_total[0].astype(jnp.bfloat16)
    value_heads = own_total[1].astype(jnp.bfloat16)
    token_q, token_k, token_v = (
        lax.all_to_all(query_heads, "seq", split_axis=0, concat_axis=1, tiled=True),
        lax.all_to_all(key_heads, "seq", split_axis=0, concat_axis=1, tiled=True),
        lax.all_to_all(value_heads, "seq", split_axis=0, concat_axis=1, tiled=True),
    )
    query_grad, query_terms = denormalize(q_values, q_inv, query_gain, token_q)
    key_grad, key_terms = denormalize(k_values, k_inv, key_gain, token_k)
    query_total, key_total_gain = lax.psum((query_terms, key_terms), ("group", "seq", "rep"))
    rep_width = feature_width // lax.axis_size("rep")
    offset = lax.axis_index("rep") * rep_width
    return (
        query_grad.reshape(query_raw.shape),
        key_grad.reshape(key_raw.shape),
        token_v.reshape(value_in.shape),
        lax.dynamic_slice_in_dim(query_total, offset, rep_width),
        lax.dynamic_slice_in_dim(key_total_gain, offset, rep_width),
    )


def solution(mesh):
    placed = (
        P("rep", "group", "seq", None),
        P("rep", "group", "seq", None),
        P("rep", "group", "seq", None),
        P("rep", "group", "seq", None),
        P(),
        P(),
        P("rep", "group"),
    )
    return jax.shard_map(
        body,
        mesh=mesh,
        in_specs=placed,
        out_specs=(
            P("rep", "group", "seq", None),
            P("rep", "group", "seq", None),
            P("rep", "group", "seq", None),
            P("rep"),
            P("rep"),
        ),
        check_vma=False,
    )
```

profile of v0, /device:TPU:0, one launch (start us, length us, event | category | flops | bytes accessed | tf_op | source)
XLA Modules:
  0.0 359.0 jit_solution(11564880806426575800)
XLA Ops:
  0.6 2.6 all_to_all.81
  4.2 4.2 %all-to-all-start.2 = ((bf16[128,2,1536]{2,0,1:T(8,128)(2,1)}), bf16[128,2,1536]{2,0,1:T(8,128)(2,1)S(1)}, u32[]{:S(2)}, u32[]{:S(2)}) async-start(bf16[128,2,1536]{2,0,1:T(8,128)(2,1)} %copy.25), calls=%async_computation.2 | async-start | bytes 1572864 | tf_op jit(solution)/shard_map/all_to_all | solution.py:67
  11.1 8.9 %all-to-all-done.2 = bf16[128,2,1536]{2,0,1:T(8,128)(2,1)S(1)} async-done(((bf16[128,2,1536]{2,0,1:T(8,128)(2,1)}), bf16[128,2,1536]{2,0,1:T(8,128)(2,1)S(1)}, u32[]{:S(2)}, u32[]{:S(2)}) %all-to-all-start.2) | async-done | bytes 786464 | tf_op jit(solution)/shard_map/all_to_all | solution.py:67
  20.0 12.9 %all_to_all.100 = bf16[128,2,1536]{2,0,1:T(8,128)(2,1)S(1)} all-to-all(bf16[128,2,1536]{2,0,1:T(8,128)(2,1)S(1)} %copy.24), channel_id=1, replica_groups=mesh['group'=4,'seq'=2,'rep'=4] {'seq'}, dimensions={1} | all-to-all | bytes 1572864 | tf_op jit(solution)/shard_map/all_to_all | solution.py:66
  33.1 2.5 collective-permute-start
  37.5 19.4 %collective-permute-start.1 = (bf16[2,256,1536]{2,1,0:T(8,128)(2,1)}, bf16[2,256,1536]{2,1,0:T(8,128)(2,1)}, u32[]{:S(2)}, u32[]{:S(2)}) collective-permute-start(bf16[2,256,1536]{2,1,0:T(8,128)(2,1)} %collective-permute-done), channel_id=1, source_target_pairs={{0,8},{8,16},{16,24},{1,9},{9,17},{17,25},{2,10},{10,18},{18,26},{... | collective-permute-start | bytes 4718600 | tf_op jit(solution)/shard_map/ppermute | solution.py:16
  56.9 2.6 all_to_all.84
  60.5 4.3 %all-to-all-start.3 = ((bf16[128,2,1536]{2,0,1:T(8,128)(2,1)}), bf16[128,2,1536]{2,0,1:T(8,128)(2,1)}, u32[]{:S(2)}, u32[]{:S(2)}) async-start(bf16[128,2,1536]{2,0,1:T(8,128)(2,1)} %copy.26), calls=%async_computation.3 | async-start | bytes 1572864 | tf_op jit(solution)/shard_map/all_to_all | solution.py:74
  68.6 2.3 copy.22
  70.9 4.7 %maximum_maximum_fusion = bf16[2,768,1536]{2,1,0:T(8,128)(2,1)} fusion(bf16[1,256,1536]{2,1,0:T(8,128)(2,1)S(1)} %bitcast.90, bf16[1,256,1536]{2,1,0:T(8,128)(2,1)S(1)} %bitcast.92, bf16[2,256,1536]{2,1,0:T(8,128)(2,1)} %collective-permute-done, bf16[2,256,1536]{2,1,0:T(8,128)(2,1)} %collective-permute-done.1), kind=kLoop, calls=%fused_computation.40 | loop fusion | flops 18874368 | bytes 9437184 | tf_op jit(solution)/shard_map/concatenate | solution.py:91
  76.7 3.5 all-to-all-start
  80.2 4.9 %slice_bitcast_fusion = (bf16[768,1536]{1,0:T(8,128)(2,1)}, bf16[768,1536]{1,0:T(8,128)(2,1)}) fusion(bf16[2,768,1536]{2,1,0:T(8,128)(2,1)} %maximum_maximum_fusion), kind=kLoop, calls=%fused_computation.47 | loop fusion | bytes 9437184 | tf_op jit(solution)/shard_map/squeeze | solution.py:93
  85.1 4.1 %all-to-all-done = bf16[128,2,1536]{2,0,1:T(8,128)(2,1)S(1)} async-done(((bf16[128,2,1536]{2,0,1:T(8,128)(2,1)}), bf16[128,2,1536]{2,0,1:T(8,128)(2,1)S(1)}, u32[]{:S(2)}, u32[]{:S(2)}) %all-to-all-start) | async-done | bytes 786464 | tf_op jit(solution)/shard_map/all_to_all | solution.py:65
  90.2 2.8 broadcast.197.clone
  92.9 2.7 broadcast.197
  95.6 106.7 %while.18 = (s32[]{:T(128)}, bf16[256,1536]{1,0:T(8,128)(2,1)}, f32[768,1536]{1,0:T(8,128)}, f32[768,1536]{1,0:T(8,128)}, bf16[256,1536]{1,0:T(8,128)(2,1)S(1)},...) while((s32[]{:T(128)}, bf16[256,1536]{1,0:T(8,128)(2,1)}, ...), condition=%wide.region_6.7_spmd.clone, body=%wide.region_2.6_spmd.clone.sunk | while | flops 255138560 | bytes 8472507 | solution.py:156
  101.3 2.2 convolution_dynamic-update-slice_fusion.2
  110.2 2.2 convolution_dynamic-update-slice_fusion.2
  137.0 2.2 convolution_dynamic-update-slice_fusion.2
  181.3 2.1 convolution_dynamic-update-slice_fusion.2
  202.4 2.2 fusion.29
  206.2 8.7 %collective-permute-done.2 = f32[2,256,1536]{2,1,0:T(8,128)S(1)} collective-permute-done((f32[2,256,1536]{2,1,0:T(8,128)S(1)}, f32[2,256,1536]{2,1,0:T(8,128)S(1)}, u32[]{:S(2)}, u32[]{:S(2)}) %collective-permute-start.2) | collective-permute-done | bytes 3145760 | tf_op jit(solution)/shard_map/ppermute | solution.py:16
  214.9 2.2 fusion.28
  218.4 3.7 %all-to-all-start.4 = ((bf16[2,128,1536]{2,1,0:T(8,128)(2,1)}), bf16[2,128,1536]{2,1,0:T(8,128)(2,1)S(1)}, u32[]{:S(2)}, u32[]{:S(2)}) async-start(bf16[2,128,1536]{2,1,0:T(8,128)(2,1)} %bitcast.15), calls=%async_computation.4 | async-start | bytes 1572864 | tf_op jit(solution)/shard_map/all_to_all | solution.py:168
  222.2 7.8 %all-to-all-done.4 = bf16[2,128,1536]{2,1,0:T(8,128)(2,1)S(1)} async-done(((bf16[2,128,1536]{2,1,0:T(8,128)(2,1)}), bf16[2,128,1536]{2,1,0:T(8,128)(2,1)S(1)}, u32[]{:S(2)}, u32[]{:S(2)}) %all-to-all-start.4) | async-done | bytes 786464 | tf_op jit(solution)/shard_map/all_to_all | solution.py:168
  233.4 23.5 %collective-permute-done.3 = f32[2,256,1536]{2,1,0:T(8,128)} collective-permute-done((f32[2,256,1536]{2,1,0:T(8,128)}, f32[2,256,1536]{2,1,0:T(8,128)}, u32[]{:S(2)}, u32[]{:S(2)}) %collective-permute-start.3) | collective-permute-done | bytes 3145760 | tf_op jit(solution)/shard_map/ppermute | solution.py:16
  256.8 3.3 fusion.31
  261.4 4.4 %all-to-all-start.5 = ((bf16[2,128,1536]{2,1,0:T(8,128)(2,1)}), bf16[2,128,1536]{2,1,0:T(8,128)(2,1)}, u32[]{:S(2)}, u32[]{:S(2)}) async-start(bf16[2,128,1536]{2,1,0:T(8,128)(2,1)} %bitcast.96), calls=%async_computation.5 | async-start | bytes 1572864 | tf_op jit(solution)/shard_map/all_to_all | solution.py:169
  267.2 2.3 copy.30
  269.5 4.4 %all-to-all-done.5 = bf16[2,128,1536]{2,1,0:T(8,128)(2,1)} async-done(((bf16[2,128,1536]{2,1,0:T(8,128)(2,1)}), bf16[2,128,1536]{2,1,0:T(8,128)(2,1)}, u32[]{:S(2)}, u32[]{:S(2)}) %all-to-all-start.5) | async-done | bytes 786464 | tf_op jit(solution)/shard_map/all_to_all | solution.py:169
  273.9 4.3 %all-to-all-start.6 = ((bf16[2,128,1536]{2,1,0:T(8,128)(2,1)}), bf16[2,128,1536]{2,1,0:T(8,128)(2,1)}, u32[]{:S(2)}, u32[]{:S(2)}) async-start(bf16[2,128,1536]{2,1,0:T(8,128)(2,1)} %bitcast.25), calls=%async_computation.6 | async-start | bytes 1572864 | tf_op jit(solution)/shard_map/all_to_all | solution.py:170
  281.7 71.1 %all-reduce = (f32[3072]{0:T(1024)S(1)}, f32[3072]{0:T(1024)S(1)}) all-reduce(f32[3072]{0:T(1024)S(1)} %reduce_sum.89, f32[3072]{0:T(1024)S(1)} %reduce_sum.91), channel_id=1, replica_groups=mesh['group'=4,'seq'=2,'rep'=4] {'group','seq','rep'}, use_global_device_ids=true, to_apply=%region_10.11 | all-reduce | flops 6144 | bytes 49152 | tf_op jit(solution)/shard_map/psum | solution.py:174
  (152 shorter events, 128.8 us)
Async XLA Ops:
  3.2 5.2 %copy-start.6 = (f32[3072]{0:T(1024)S(1)}, f32[3072]{0:T(1024)}, u32[]{:S(2)}) copy-start(f32[3072]{0:T(1024)} %param.14) | copy-start | bytes 36868
  3.2 5.2 %copy-start.4 = (bf16[1,1,128,3072]{3,2,1,0:T(8,128)(2,1)S(1)}, bf16[1,1,128,3072]{3,2,1,0:T(8,128)(2,1)}, u32[]{:S(2)}) copy-start(bf16[1,1,128,3072]{3,2,1,0:T(8,128)(2,1)} %param.10) | copy-start | bytes 2359300
  4.2 15.8 %all-to-all-start.2 = ((bf16[128,2,1536]{2,0,1:T(8,128)(2,1)}), bf16[128,2,1536]{2,0,1:T(8,128)(2,1)S(1)}, u32[]{:S(2)}, u32[]{:S(2)}) async-start(bf16[128,2,1536]{2,0,1:T(8,128)(2,1)} %copy.25), calls=%async_computation.2 | async-start | bytes 1572864 | tf_op jit(solution)/shard_map/all_to_all | solution.py:67
  33.1 4.4 %collective-permute-start = (bf16[2,256,1536]{2,1,0:T(8,128)(2,1)S(1)}, bf16[2,256,1536]{2,1,0:T(8,128)(2,1)}, u32[]{:S(2)}, u32[]{:S(2)}) collective-permute-start(bf16[2,256,1536]{2,1,0:T(8,128)(2,1)S(1)} %pad_maximum_fusion.1), channel_id=1, source_target_pairs={{0,8},{8,16},{16,24},{1,9},{9,17},{17,25},{2,10},{10,18},{18,26},{... | collective-permute-start | bytes 4718600 | tf_op jit(solution)/shard_map/ppermute | solution.py:16
  37.5 33.4 %collective-permute-start.1 = (bf16[2,256,1536]{2,1,0:T(8,128)(2,1)}, bf16[2,256,1536]{2,1,0:T(8,128)(2,1)}, u32[]{:S(2)}, u32[]{:S(2)}) collective-permute-start(bf16[2,256,1536]{2,1,0:T(8,128)(2,1)} %collective-permute-done), channel_id=1, source_target_pairs={{0,8},{8,16},{16,24},{1,9},{9,17},{17,25},{2,10},{10,18},{18,26},{... | collective-permute-start | bytes 4718600 | tf_op jit(solution)/shard_map/ppermute | solution.py:16
  59.5 5.3 %copy-start.5 = (f32[3072]{0:T(1024)S(1)}, f32[3072]{0:T(1024)}, u32[]{:S(2)}) copy-start(f32[3072]{0:T(1024)} %param.13) | copy-start | bytes 36868
  60.5 16.2 %all-to-all-start.3 = ((bf16[128,2,1536]{2,0,1:T(8,128)(2,1)}), bf16[128,2,1536]{2,0,1:T(8,128)(2,1)}, u32[]{:S(2)}, u32[]{:S(2)}) async-start(bf16[128,2,1536]{2,0,1:T(8,128)(2,1)} %copy.26), calls=%async_computation.3 | async-start | bytes 1572864 | tf_op jit(solution)/shard_map/all_to_all | solution.py:74
  76.7 12.6 %all-to-all-start = ((bf16[128,2,1536]{2,0,1:T(8,128)(2,1)}), bf16[128,2,1536]{2,0,1:T(8,128)(2,1)S(1)}, u32[]{:S(2)}, u32[]{:S(2)}) async-start(bf16[128,2,1536]{2,0,1:T(8,128)(2,1)} %copy.22), calls=%async_computation | async-start | bytes 1572864 | tf_op jit(solution)/shard_map/all_to_all | solution.py:65
  202.4 12.6 %slice-start = ((s8[4718592]{0:T(1024)(128)(4,1)}), s8[4194304]{0:T(1024)(128)(4,1)S(1)}, s32[]{:S(2)}) async-start(s8[4718592]{0:T(1024)(128)(4,1)} %bitcast.81), calls=%async_computation.7 | async-start | bytes 8388608
  202.4 12.6 %slice-start.1 = ((s8[4718592]{0:T(1024)(128)(4,1)}), s8[524288]{0:T(1024)(128)(4,1)S(1)}, s32[]{:S(2)}) async-start(s8[4718592]{0:T(1024)(128)(4,1)} %bitcast.81), calls=%async_computation.8 | async-start | bytes 1048576
  202.4 12.6 %copy-start = (f32[768,1536]{1,0:T(8,128)S(1)}, f32[768,1536]{1,0:T(8,128)}, u32[]{:S(2)}) copy-start(f32[768,1536]{1,0:T(8,128)} %get-tuple-element.162) | copy-start | bytes 14155780
  204.6 10.3 %collective-permute-start.2 = (f32[2,256,1536]{2,1,0:T(8,128)S(1)}, f32[2,256,1536]{2,1,0:T(8,128)S(1)}, u32[]{:S(2)}, u32[]{:S(2)}) collective-permute-start(f32[2,256,1536]{2,1,0:T(8,128)S(1)} %fusion.29), channel_id=1, source_target_pairs={{8,0},{16,8},{24,16},{9,1},{17,9},{25,17},{10,2},{18,10},{26,18},{... | collective-permute-start | bytes 9437192 | tf_op jit(solution)/shard_map/ppermute | solution.py:16
  217.2 39.7 %collective-permute-start.3 = (f32[2,256,1536]{2,1,0:T(8,128)}, f32[2,256,1536]{2,1,0:T(8,128)}, u32[]{:S(2)}, u32[]{:S(2)}) collective-permute-start(f32[2,256,1536]{2,1,0:T(8,128)} %fusion.28), channel_id=1, source_target_pairs={{8,0},{16,8},{24,16},{9,1},{17,9},{25,17},{10,2},{18,10},{26,18},{... | collective-permute-start | bytes 9437192 | tf_op jit(solution)/shard_map/ppermute | solution.py:16
  218.4 11.5 %all-to-all-start.4 = ((bf16[2,128,1536]{2,1,0:T(8,128)(2,1)}), bf16[2,128,1536]{2,1,0:T(8,128)(2,1)S(1)}, u32[]{:S(2)}, u32[]{:S(2)}) async-start(bf16[2,128,1536]{2,1,0:T(8,128)(2,1)} %bitcast.15), calls=%async_computation.4 | async-start | bytes 1572864 | tf_op jit(solution)/shard_map/all_to_all | solution.py:168
  230.3 2.0 copy-start.3
  261.4 4.5 %copy-start.1 = (f32[2,128,1536]{1,2,0:T(8,128)S(1)}, f32[2,128,1536]{1,2,0:T(8,128)}, u32[]{:S(2)}) copy-start(f32[2,128,1536]{1,2,0:T(8,128)} %convert_element_type.166) | copy-start | bytes 4718596
  261.4 12.5 %all-to-all-start.5 = ((bf16[2,128,1536]{2,1,0:T(8,128)(2,1)}), bf16[2,128,1536]{2,1,0:T(8,128)(2,1)}, u32[]{:S(2)}, u32[]{:S(2)}) async-start(bf16[2,128,1536]{2,1,0:T(8,128)(2,1)} %bitcast.96), calls=%async_computation.5 | async-start | bytes 1572864 | tf_op jit(solution)/shard_map/all_to_all | solution.py:169
  273.9 80.7 %all-to-all-start.6 = ((bf16[2,128,1536]{2,1,0:T(8,128)(2,1)}), bf16[2,128,1536]{2,1,0:T(8,128)(2,1)}, u32[]{:S(2)}, u32[]{:S(2)}) async-start(bf16[2,128,1536]{2,1,0:T(8,128)(2,1)} %bitcast.25), calls=%async_computation.6 | async-start | bytes 1572864 | tf_op jit(solution)/shard_map/all_to_all | solution.py:170
  279.7 1.4 copy-start.2
where the time goes:
time: 362 us; the launch traced here: 359 us
  matrix products  92.3 us (25%)
  blocking collectives  84.1 us (23%)
  waiting for transfers between devices  60.5 us (17%)
  starting transfers between devices  49.3 us (14%)
  other arithmetic  36.2 us (10%)
  local copies, waits for them, and re-layouts  35.5 us (10%)
    psum x1, blocking collectives, body(): lax.psum((query_terms, key_terms), ('group', 'seq', 'rep'))  71.1 us
    ppermute x4, waiting for transfers between devices, from_behind(): return lax.ppermute(block, axis, route)  34.2 us
    dot_general x12, matrix products, head_pass(): jnp.dot(probs_low.T, cot_head, preferred_element_type=jnp.float32)  25.6 us
    ppermute x4, starting transfers between devices, from_behind(): return lax.ppermute(block, axis, route)  24.7 us
    dot_general x12, matrix products, head_pass(): jnp.dot(dscores, key_head, preferred_element_type=jnp.float32) * factor  21.8 us
    dot_general x12, matrix products, head_pass(): dprobs = jnp.dot(cot_head, value_head.T, preferred_element_type=jnp.float32)  16.1 us
    dot_general x12, matrix products, head_pass(): jnp.dot(query_head, key_head.T, preferred_element_type=jnp.float32) * factor  15.4 us
    dot_general x12, matrix products, head_pass(): jnp.dot(dscores.T, query_head, preferred_element_type=jnp.float32) * factor  13.3 us
  transfers between devices with their start and end apart: 10, of which 8 were waited for; matrix products, arithmetic and copies ran while one was open for 8% of the time, Pallas kernels for 0%

commit v1 on v0

--- a/solution.py
+++ b/solution.py
@@ -1,6 +1,10 @@
+import functools
+
 import jax
 import jax.numpy as jnp
 from jax import lax
+from jax.experimental import pallas as pl
+from jax.experimental.pallas import tpu as pltpu
 from jax.sharding import PartitionSpec as P
 
 HEAD_DIM = 128
@@ -56,7 +60,331 @@
     return from_behind(cotangent_pair, "group", hop_count)
 
 
-def body(query_raw, key_raw, value_in, out_cotangent, query_gain, key_gain, attend_from):
+MESH = pl.DeviceIdType.MESH
+ROWS = 16
+NT = (((1,), (1,)), ((), ()))
+
+
+def dot(left, right, dims=(((1,), (0,)), ((), ()))):
+    return lax.dot_general(left, right, dims, preferred_element_type=jnp.float32)
+
+
+def head_kernel(
+    sizes,
+    attend_ref, q_hbm, k_hbm, v_hbm, c_hbm, q_gain, k_gain,
+    q_out, k_out, v_out, q_gain_out, k_gain_out,
+    raw, normed, inv, heads, grads, back, first, acc, terms, gathered,
+    raw_sem, send_sem, recv_sem, own_sem, back_send, back_recv, back_own,
+    first_send, first_recv, terms_send, terms_recv,
+):
+    groups, seqs, reps, tokens, width, per_owner = sizes
+    owners = groups * seqs
+    group_len = seqs * tokens
+    own_width = per_owner * HEAD_DIM
+    per_rep = owners // reps
+    group, seq, rep = lax.axis_index("group"), lax.axis_index("seq"), lax.axis_index("rep")
+    me = group * seqs + seq
+    factor = HEAD_DIM ** (-0.5)
+
+    loads = []
+    for which, source in enumerate((q_hbm, k_hbm)):
+        load = pltpu.make_async_copy(source, raw.at[which], raw_sem.at[which])
+        load.start()
+        loads.append(load)
+
+    barrier = pltpu.get_barrier_semaphore()
+    devices = owners * reps
+    flat = me * reps + rep
+
+    def greet(step, carry):
+        other = lax.rem(flat + step, devices)
+        place = {
+            "group": other // (seqs * reps),
+            "seq": lax.rem(other // reps, seqs),
+            "rep": lax.rem(other, reps),
+        }
+        pl.semaphore_signal(barrier, inc=1, device_id=place, device_id_type=MESH)
+        return carry
+
+    lax.fori_loop(1, devices, greet, 0)
+
+    def partner(step):
+        other = lax.rem(me + step, owners)
+        return other, {"group": other // seqs, "seq": lax.rem(other, seqs)}
+
+    my_rows = pl.ds(pl.multiple_of(me * tokens, tokens), tokens)
+
+    def columns(owner, head):
+        return pl.ds(pl.multiple_of(owner * own_width + head * HEAD_DIM, HEAD_DIM), HEAD_DIM)
+
+    def send_heads(which, source, head):
+        for step in range(1, owners):
+            other, place = partner(step)
+            pltpu.make_async_remote_copy(
+                src_ref=source.at[:, columns(other, head)],
+                dst_ref=heads.at[which, head, my_rows],
+                send_sem=send_sem.at[which, head],
+                recv_sem=recv_sem.at[which, head],
+                device_id=place,
+                device_id_type=MESH,
+            ).start()
+        pltpu.make_async_copy(
+            source.at[:, columns(me, head)], heads.at[which, head, my_rows], recv_sem.at[which, head]
+        ).start()
+
+    def normalize_rows(which, gain_ref):
+        def step(index, carry):
+            rows = pl.ds(pl.multiple_of(index * ROWS, ROWS), ROWS)
+            values = raw[which, rows, :].astype(jnp.float32)
+            scale = lax.rsqrt(jnp.mean(values * values, axis=-1, keepdims=True) + EPSILON)
+            inv[which, rows, :] = scale
+            normed[which, rows, :] = (values * scale * gain_ref[...]).astype(jnp.bfloat16)
+            return carry
+
+        lax.fori_loop(0, tokens // ROWS, step, 0)
+
+    first[me] = jnp.full(first.shape[1:], attend_ref[0, 0].astype(jnp.float32))
+    pl.semaphore_wait(barrier, devices - 1)
+    for step in range(1, owners):
+        other, place = partner(step)
+        pltpu.make_async_remote_copy(
+            src_ref=first.at[me],
+            dst_ref=first.at[me],
+            send_sem=first_send,
+            recv_sem=first_recv,
+            device_id=place,
+            device_id_type=MESH,
+        ).start()
+    send_heads(2, v_hbm, 0)
+    send_heads(3, c_hbm, 0)
+    loads[0].wait()
+    normalize_rows(0, q_gain)
+    send_heads(0, normed.at[0], 0)
+    loads[1].wait()
+    normalize_rows(1, k_gain)
+    send_heads(1, normed.at[1], 0)
+
+    def send_rest(head, carry):
+        for which, source in ((0, normed.at[0]), (1, normed.at[1]), (2, v_hbm), (3, c_hbm)):
+            send_heads(which, source, head)
+        return carry
+
+    lax.fori_loop(1, per_owner, send_rest, 0)
+
+    terms[...] = jnp.zeros(terms.shape, jnp.float32)
+    few = first.at[pl.ds(0, owners - 1)]
+    pltpu.make_async_copy(few, few, first_recv).wait()
+
+    def one_head(head, carry):
+        for which in range(4):
+            whole = heads.at[which, head]
+            pltpu.make_async_copy(whole, whole, recv_sem.at[which, head]).wait()
+
+        def block(which, index):
+            return heads[which, head, index * group_len : (index + 1) * group_len, :]
+
+        turned = [jnp.transpose(block(1, index)) for index in range(groups)]
+        q_terms = jnp.zeros((1, HEAD_DIM), jnp.float32)
+        k_terms = jnp.zeros((1, HEAD_DIM), jnp.float32)
+        for group_at in range(groups):
+            low = max(0, group_at - PAST)
+            window = range(low, group_at + 1)
+            q_block, c_block = block(0, group_at), block(3, group_at)
+            first_row = first[group_at * seqs, 0:1, :]
+            scores = []
+            for index in window:
+                score = dot(block(1, index), q_block, NT) * factor
+                if index < group_at:
+                    score = score + jnp.where(first_row > index, -1e30, 0.0)
+                scores.append(score)
+            top = functools.reduce(
+                jnp.maximum, [jnp.max(score, axis=0, keepdims=True) for score in scores]
+            )
+            weights = [jnp.exp(score - top) for score in scores]
+            total = sum(jnp.sum(weight, axis=0, keepdims=True) for weight in weights)
+            share = 1.0 / total
+            probs = [weight * share for weight in weights]
+            dprobs = [dot(block(2, index), c_block, NT) for index in window]
+            delta = sum(
+                jnp.sum(prob * dprob, axis=0, keepdims=True) for prob, dprob in zip(probs, dprobs)
+            )
+            q_turned = jnp.zeros((HEAD_DIM, group_len), jnp.float32)
+            for index, prob, dprob in zip(window, probs, dprobs):
+                rows = slice(index * group_len, (index + 1) * group_len)
+                dscore = (prob * (dprob - delta)).astype(jnp.bfloat16)
+                k_part = dot(dscore, q_block)
+                v_part = dot(prob.astype(jnp.bfloat16), c_block)
+                if index < group_at:
+                    k_part = k_part + acc[0, rows, :]
+                    v_part = v_part + acc[1, rows, :]
+                if group_at == min(index + PAST, groups - 1):
+                    k_low = (k_part * factor).astype(jnp.bfloat16)
+                    grads[1, head, rows, :] = k_low
+                    grads[2, head, rows, :] = v_part.astype(jnp.bfloat16)
+                    k_terms = k_terms + jnp.sum(
+                        k_low.astype(jnp.float32) * block(1, index).astype(jnp.float32),
+                        axis=0,
+                        keepdims=True,
+                    )
+                else:
+                    acc[0, rows, :] = k_part
+                    acc[1, rows, :] = v_part
+                q_turned = q_turned + dot(turned[index], dscore)
+            q_low = (jnp.transpose(q_turned) * factor).astype(jnp.bfloat16)
+            grads[0, head, group_at * group_len : (group_at + 1) * group_len, :] = q_low
+            q_terms = q_terms + jnp.sum(
+                q_low.astype(jnp.float32) * q_block.astype(jnp.float32), axis=0, keepdims=True
+            )
+        terms[head, 0:1, :] = q_terms / q_gain[:, columns(me, head)]
+        terms[head, 1:2, :] = k_terms / k_gain[:, columns(me, head)]
+        for which, landing in ((0, back.at[0]), (1, back.at[1]), (2, v_out)):
+            for step in range(1, owners):
+                other, place = partner(step)
+                pltpu.make_async_remote_copy(
+                    src_ref=grads.at[which, head, pl.ds(pl.multiple_of(other * tokens, tokens), tokens)],
+                    dst_ref=landing.at[:, columns(me, head)],
+                    send_sem=back_send.at[which],
+                    recv_sem=back_recv.at[which],
+                    device_id=place,
+                    device_id_type=MESH,
+                ).start()
+            pltpu.make_async_copy(
+                grads.at[which, head, my_rows], landing.at[:, columns(me, head)], back_recv.at[which]
+            ).start()
+        return carry
+
+    lax.fori_loop(0, per_owner, one_head, 0)
+
+    target_rep = me // per_rep
+    slot = rep * per_rep + lax.rem(me, per_rep)
+
+    def send_terms(place):
+        pltpu.make_async_remote_copy(
+            src_ref=terms,
+            dst_ref=gathered.at[slot],
+            send_sem=terms_send,
+            recv_sem=terms_recv,
+            device_id={**place, "rep": target_rep},
+            device_id_type=MESH,
+        ).start()
+
+    for step in range(1, owners):
+        send_terms(partner(step)[1])
+
+    @pl.when(rep != target_rep)
+    def _():
+        send_terms(partner(0)[1])
+
+    @pl.when(rep == target_rep)
+    def _():
+        pltpu.make_async_copy(terms, gathered.at[slot], terms_recv).start()
+
+    def denormalize_rows(which, gain_ref, out_ref):
+        def step(index, carry):
+            rows = pl.ds(pl.multiple_of(index * ROWS, ROWS), ROWS)
+            values = raw[which, rows, :].astype(jnp.float32)
+            scale = inv[which, rows, :]
+            weighted = back[which, rows, :].astype(jnp.float32) * gain_ref[...]
+            inner = jnp.mean(values * weighted, axis=-1, keepdims=True)
+            result = scale * weighted - values * (scale * scale * scale * inner)
+            out_ref[rows, :] = result.astype(jnp.bfloat16)
+            return carry
+
+        lax.fori_loop(0, tokens // ROWS, step, 0)
+
+    for which, gain_ref, out_ref in ((0, q_gain, q_out), (1, k_gain, k_out)):
+        pltpu.make_async_copy(back.at[which], back.at[which], back_recv.at[which]).wait()
+        denormalize_rows(which, gain_ref, out_ref)
+
+    pltpu.make_async_copy(gathered, gathered, terms_recv).wait()
+    for sub in range(per_rep):
+        for head in range(per_owner):
+            lanes = slice((sub * per_owner + head) * HEAD_DIM, (sub * per_owner + head + 1) * HEAD_DIM)
+            sums = sum(gathered[clip * per_rep + sub, head] for clip in range(reps))
+            q_gain_out[:, lanes] = sums[0:1]
+            k_gain_out[:, lanes] = sums[1:2]
+    pltpu.make_async_copy(v_out, v_out, back_recv.at[2]).wait()
+
+    pltpu.make_async_copy(few, few, first_send).wait()
+    for which in range(4):
+        for head in range(per_owner):
+            sent = heads.at[which, head, pl.ds(0, (owners - 1) * tokens)]
+            pltpu.make_async_copy(sent, sent, send_sem.at[which, head]).wait()
+    for which in range(3):
+        sent = grads.at[which, :, pl.ds(0, (owners - 1) * tokens)]
+        pltpu.make_async_copy(sent, sent, back_send.at[which]).wait()
+    sent = gathered.at[pl.ds(0, owners - 1)]
+    pltpu.make_async_copy(sent, sent, terms_send).wait()
+
+    @pl.when(rep != target_rep)
+    def _():
+        pltpu.make_async_copy(terms, terms, terms_send).wait()
+
+
+def head_body(query_raw, key_raw, value_in, out_cotangent, query_gain, key_gain, attend_from):
+    groups, seqs, reps = (lax.axis_size(name) for name in ("group", "seq", "rep"))
+    tokens, width = query_raw.shape[2:]
+    owners = groups * seqs
+    per_owner = width // HEAD_DIM // owners
+    group_len = seqs * tokens
+    clip_len = owners * tokens
+    low = jnp.bfloat16
+    rows = jax.ShapeDtypeStruct((tokens, width), low)
+    gain_rows = jax.ShapeDtypeStruct((1, width // reps), jnp.float32)
+    vmem = pl.BlockSpec(memory_space=pltpu.VMEM)
+    hbm = pl.BlockSpec(memory_space=pl.ANY)
+    dma = pltpu.SemaphoreType.DMA
+    sizes = (groups, seqs, reps, tokens, width, per_owner)
+    q_grad, k_grad, v_grad, q_gain_grad, k_gain_grad = pl.pallas_call(
+        functools.partial(head_kernel, sizes),
+        out_shape=(rows, rows, rows, gain_rows, gain_rows),
+        in_specs=[pl.BlockSpec(memory_space=pltpu.SMEM)] + [hbm] * 4 + [vmem] * 2,
+        out_specs=(vmem,) * 5,
+        scratch_shapes=[
+            pltpu.VMEM((2, tokens, width), low),
+            pltpu.VMEM((2, tokens, width), low),
+            pltpu.VMEM((2, tokens, 1), jnp.float32),
+            pltpu.VMEM((4, per_owner, clip_len, HEAD_DIM), low),
+            pltpu.VMEM((3, per_owner, clip_len, HEAD_DIM), low),
+            pltpu.VMEM((2, tokens, width), low),
+            pltpu.VMEM((owners, 8, group_len), jnp.float32),
+            pltpu.VMEM((2, clip_len, HEAD_DIM), jnp.float32),
+            pltpu.VMEM((per_owner, 8, HEAD_DIM), jnp.float32),
+            pltpu.VMEM((owners, per_owner, 8, HEAD_DIM), jnp.float32),
+            dma((2,)),
+            dma((4, per_owner)),
+            dma((4, per_owner)),
+            dma,
+            dma((3,)),
+            dma((3,)),
+            dma,
+            dma,
+            dma,
+            dma,
+            dma,
+        ],
+        compiler_params=pltpu.CompilerParams(
+            collective_id=0, has_side_effects=True, vmem_limit_bytes=48 * 1024 * 1024
+        ),
+    )(
+        attend_from,
+        query_raw.reshape(tokens, width),
+        key_raw.reshape(tokens, width),
+        value_in.reshape(tokens, width),
+        out_cotangent.reshape(tokens, width),
+        query_gain.reshape(1, width),
+        key_gain.reshape(1, width),
+    )
+    return (
+        q_grad.reshape(query_raw.shape),
+        k_grad.reshape(key_raw.shape),
+        v_grad.reshape(value_in.shape),
+        q_gain_grad.reshape(-1),
+        k_gain_grad.reshape(-1),
+    )
+
+
+def ring_body(query_raw, key_raw, value_in, out_cotangent, query_gain, key_gain, attend_from):
     tok_rows = query_raw.shape[2]
     feature_width = query_raw.shape[3]
     q_values, q_inv, q_normed = normalize(query_raw.reshape(tok_rows, feature_width), query_gain)
@@ -183,6 +511,16 @@
     )
 
 
+def body(*arrays):
+    tokens, width = arrays[0].shape[2:]
+    owners = lax.axis_size("group") * lax.axis_size("seq")
+    heads = width // HEAD_DIM
+    even = heads % owners == 0 and owners % lax.axis_size("rep") == 0
+    if even and tokens * owners * heads <= 32768 and tokens % 16 == 0:
+        return head_body(*arrays)
+    return ring_body(*arrays)
+
+
 def solution(mesh):
     placed = (
         P("rep", "group", "seq", None),

time: 362 us -> 82.3 us (0.23)
  matrix products: 92.3 us -> 0 us
  blocking collectives: 84.1 us -> 0 us
  Pallas kernels: 0 us -> 71.5 us
  waiting for transfers between devices: 60.5 us -> 0 us
  starting transfers between devices: 49.3 us -> 0 us
  other arithmetic: 36.2 us -> 1.21 us
  local copies, waits for them, and re-layouts: 35.5 us -> 7.92 us
    dot_general x60 -> x0, matrix products: 92.3 us -> none  [the longest x12 25.6 us: head_pass(): jnp.dot(probs_low.T, cot_head, preferred_element_type=jnp.float32)]
    pallas_call x0 -> x1, Pallas kernels: none -> 71.5 us  [head_body(): pl.pallas_call(functools.partial(head_kernel, sizes), out_shape=(rows, ro...]
    psum x1 -> x0, blocking collectives: 71.1 us -> none  [body(): lax.psum((query_terms, key_terms), ('group', 'seq', 'rep'))]
    ppermute x4 -> x0, waiting for transfers between devices: 34.2 us -> none  [from_behind(): return lax.ppermute(block, axis, route)]
    all_to_all x6 -> x0, waiting for transfers between devices: 26.3 us -> none  [the longest x1 8.92 us: body(): lax.all_to_all(value_in.reshape(tok_rows, feature_width), 'seq', split_ax...]
    ppermute x4 -> x0, starting transfers between devices: 24.7 us -> none  [from_behind(): return lax.ppermute(block, axis, route)]
    all_to_all x6 -> x0, starting transfers between devices: 24.5 us -> none  [the longest x1 4.45 us: body(): lax.all_to_all(key_heads, 'seq', split_axis=0, concat_axis=1, tiled=True)]
    all_to_all x1 -> x0, blocking collectives: 12.9 us -> none  [body(): lax.all_to_all(k_normed, 'seq', split_axis=1, concat_axis=0, tiled=True)]
  transfers between devices with their start and end apart: 10 -> 0, of which waited for: 8 -> 0; matrix products, arithmetic and copies ran while one was open for 8% -> 0% of each run, Pallas kernels for 0% -> 0%
where the time goes in v1:
time: 82.3 us; the launch traced here: 81.9 us
  Pallas kernels  71.5 us (87%)
  local copies, waits for them, and re-layouts  7.92 us (10%)
  between operations  1.32 us (2%)
  other arithmetic  1.21 us (1%)
    pallas_call x1, Pallas kernels, head_body(): pl.pallas_call(functools.partial(head_kernel, sizes), out_shape=(rows, ro...  71.5 us
    unnamed x15, local copies, waits for them, and re-layouts  7.92 us

profile of v1, /device:TPU:0, one launch (start us, length us, event | category | flops | bytes accessed | tf_op | source)
XLA Modules:
  0.0 81.9 jit_solution(2957749177973630679)
XLA Ops:
  0.6 0.0 copy-start.4
  1.3 0.0 copy-done.4
  1.3 0.0 copy-start
  1.3 1.1 %copy-done = bf16[1,1,128,3072]{3,2,1,0:T(8,128)(2,1)S(1)} copy-done((bf16[1,1,128,3072]{3,2,1,0:T(8,128)(2,1)S(1)}, bf16[1,1,128,3072]{3,2,1,0:T(8,128)(2,1)}, u32[]{:S(2)}) %copy-start) | copy-done | bytes 786456
  2.5 0.0 copy-start.1
  2.5 1.1 %copy-done.1 = bf16[1,1,128,3072]{3,2,1,0:T(8,128)(2,1)S(1)} copy-done((bf16[1,1,128,3072]{3,2,1,0:T(8,128)(2,1)S(1)}, bf16[1,1,128,3072]{3,2,1,0:T(8,128)(2,1)}, u32[]{:S(2)}) %copy-start.1) | copy-done | bytes 786456
  3.6 0.0 copy-start.2
  3.6 1.1 %copy-done.2 = bf16[1,1,128,3072]{3,2,1,0:T(8,128)(2,1)S(1)} copy-done((bf16[1,1,128,3072]{3,2,1,0:T(8,128)(2,1)S(1)}, bf16[1,1,128,3072]{3,2,1,0:T(8,128)(2,1)}, u32[]{:S(2)}) %copy-start.2) | copy-done | bytes 786456
  4.7 0.0 copy-start.3
  4.7 1.1 %copy-done.3 = bf16[1,1,128,3072]{3,2,1,0:T(8,128)(2,1)S(1)} copy-done((bf16[1,1,128,3072]{3,2,1,0:T(8,128)(2,1)S(1)}, bf16[1,1,128,3072]{3,2,1,0:T(8,128)(2,1)}, u32[]{:S(2)}) %copy-start.3) | copy-done | bytes 786456
  5.9 0.0 copy-start.5
  5.9 0.7 copy-done.5
  6.6 71.5 %shard_map.110 = (bf16[128,3072]{1,0:T(8,128)(2,1)S(1)}, bf16[128,3072]{1,0:T(8,128)(2,1)S(1)}, bf16[128,3072]{1,0:T(8,128)(2,1)S(1)}, f32[1,768]{1,0:T(1,128)S(1)}, f32[1,768]{1,0:T(1,128)S(1)}) custom-call(s32[1,1]{1,0:T(1,128)S(6)} %copy.15.attend_ref, bf16[128,3072]{1,0:T(8,128)(2,1)S(1)} %bitcast.12, bf16[128,3072]{1,0:T(8,128)(2,1)S(1)} %bitcast.13, ...), custom_call_target="tpu_custom_call" | custom-call | tf_op jit(solution)/shard_map/pallas_call | solution.py:338
  78.1 0.6 reduce
  78.7 0.6 reduce.1
  79.3 0.9 %copy.16 = bf16[1,1,128,3072]{3,2,1,0:T(8,128)(2,1)} copy(bf16[1,1,128,3072]{3,2,1,0:T(8,128)(2,1)S(1)} %bitcast.11) | data formatting | bytes 1572864
  80.1 0.9 %copy.17 = bf16[1,1,128,3072]{3,2,1,0:T(8,128)(2,1)} copy(bf16[1,1,128,3072]{3,2,1,0:T(8,128)(2,1)S(1)} %bitcast.10) | data formatting | bytes 1572864
  81.0 0.9 %copy.18 = bf16[1,1,128,3072]{3,2,1,0:T(8,128)(2,1)} copy(bf16[1,1,128,3072]{3,2,1,0:T(8,128)(2,1)S(1)} %bitcast.9) | data formatting | bytes 1572864
Async XLA Ops:
  0.6 0.7 copy-start.4
  1.3 1.1 %copy-start = (bf16[1,1,128,3072]{3,2,1,0:T(8,128)(2,1)S(1)}, bf16[1,1,128,3072]{3,2,1,0:T(8,128)(2,1)}, u32[]{:S(2)}) copy-start(bf16[1,1,128,3072]{3,2,1,0:T(8,128)(2,1)} %param.7) | copy-start | bytes 2359300
  2.5 1.1 %copy-start.1 = (bf16[1,1,128,3072]{3,2,1,0:T(8,128)(2,1)S(1)}, bf16[1,1,128,3072]{3,2,1,0:T(8,128)(2,1)}, u32[]{:S(2)}) copy-start(bf16[1,1,128,3072]{3,2,1,0:T(8,128)(2,1)} %param.8) | copy-start | bytes 2359300
  3.6 1.1 %copy-start.2 = (bf16[1,1,128,3072]{3,2,1,0:T(8,128)(2,1)S(1)}, bf16[1,1,128,3072]{3,2,1,0:T(8,128)(2,1)}, u32[]{:S(2)}) copy-start(bf16[1,1,128,3072]{3,2,1,0:T(8,128)(2,1)} %param.9) | copy-start | bytes 2359300
  4.7 1.1 %copy-start.3 = (bf16[1,1,128,3072]{3,2,1,0:T(8,128)(2,1)S(1)}, bf16[1,1,128,3072]{3,2,1,0:T(8,128)(2,1)}, u32[]{:S(2)}) copy-start(bf16[1,1,128,3072]{3,2,1,0:T(8,128)(2,1)} %param.10) | copy-start | bytes 2359300
  5.9 0.7 copy-start.5

commit v2 on v1

--- a/solution.py
+++ b/solution.py
@@ -62,6 +62,7 @@
 
 MESH = pl.DeviceIdType.MESH
 ROWS = 16
+STORE_PARTS = 4
 NT = (((1,), (1,)), ((), ()))
 
 
@@ -74,7 +75,7 @@
     attend_ref, q_hbm, k_hbm, v_hbm, c_hbm, q_gain, k_gain,
     q_out, k_out, v_out, q_gain_out, k_gain_out,
     raw, normed, inv, heads, grads, back, first, acc, terms, gathered,
-    raw_sem, send_sem, recv_sem, own_sem, back_send, back_recv, back_own,
+    raw_sem, send_sem, recv_sem, back_send, back_recv,
     first_send, first_recv, terms_send, terms_recv,
 ):
     groups, seqs, reps, tokens, width, per_owner = sizes
@@ -301,8 +302,8 @@
         for head in range(per_owner):
             lanes = slice((sub * per_owner + head) * HEAD_DIM, (sub * per_owner + head + 1) * HEAD_DIM)
             sums = sum(gathered[clip * per_rep + sub, head] for clip in range(reps))
-            q_gain_out[:, lanes] = sums[0:1]
-            k_gain_out[:, lanes] = sums[1:2]
+            q_gain_out[lanes] = sums[0]
+            k_gain_out[lanes] = sums[1]
     pltpu.make_async_copy(v_out, v_out, back_recv.at[2]).wait()
 
     pltpu.make_async_copy(few, few, first_send).wait()
@@ -321,6 +322,23 @@
         pltpu.make_async_copy(terms, terms, terms_send).wait()
 
 
+def store_kernel(*refs):
+    sources, targets, sems = refs[:5], refs[5:10], refs[10]
+    copies = []
+    for which, (source, target) in enumerate(zip(sources, targets)):
+        parts = STORE_PARTS if len(source.shape) == 2 else 1
+        step = source.shape[0] // parts
+        for part in range(parts):
+            piece = pl.ds(part * step, step)
+            copies.append(
+                pltpu.make_async_copy(source.at[piece], target.at[piece], sems.at[which, part])
+            )
+    for copy in copies:
+        copy.start()
+    for copy in copies:
+        copy.wait()
+
+
 def head_body(query_raw, key_raw, value_in, out_cotangent, query_gain, key_gain, attend_from):
     groups, seqs, reps = (lax.axis_size(name) for name in ("group", "seq", "rep"))
     tokens, width = query_raw.shape[2:]
@@ -330,12 +348,13 @@
     clip_len = owners * tokens
     low = jnp.bfloat16
     rows = jax.ShapeDtypeStruct((tokens, width), low)
-    gain_rows = jax.ShapeDtypeStruct((1, width // reps), jnp.float32)
+    gain_rows = jax.ShapeDtypeStruct((width // reps,), jnp.float32)
     vmem = pl.BlockSpec(memory_space=pltpu.VMEM)
-    hbm = pl.BlockSpec(memory_space=pl.ANY)
+    hbm = pl.BlockSpec(memory_space=pltpu.HBM)
+    anywhere = pl.BlockSpec(memory_space=pl.ANY)
     dma = pltpu.SemaphoreType.DMA
     sizes = (groups, seqs, reps, tokens, width, per_owner)
-    q_grad, k_grad, v_grad, q_gain_grad, k_gain_grad = pl.pallas_call(
+    results = pl.pallas_call(
         functools.partial(head_kernel, sizes),
         out_shape=(rows, rows, rows, gain_rows, gain_rows),
         in_specs=[pl.BlockSpec(memory_space=pltpu.SMEM)] + [hbm] * 4 + [vmem] * 2,
@@ -354,17 +373,15 @@
             dma((2,)),
             dma((4, per_owner)),
             dma((4, per_owner)),
-            dma,
             dma((3,)),
             dma((3,)),
             dma,
             dma,
             dma,
             dma,
-            dma,
         ],
         compiler_params=pltpu.CompilerParams(
-            collective_id=0, has_side_effects=True, vmem_limit_bytes=48 * 1024 * 1024
+            collective_id=0, has_side_effects=True, vmem_limit_bytes=57 * 1024 * 1024
         ),
     )(
         attend_from,
@@ -375,12 +392,19 @@
         query_gain.reshape(1, width),
         key_gain.reshape(1, width),
     )
+    q_grad, k_grad, v_grad, q_gain_grad, k_gain_grad = pl.pallas_call(
+        store_kernel,
+        out_shape=(rows, rows, rows, gain_rows, gain_rows),
+        in_specs=[vmem] * 5,
+        out_specs=(anywhere,) * 5,
+        scratch_shapes=[dma((5, STORE_PARTS))],
+    )(*results)
     return (
         q_grad.reshape(query_raw.shape),
         k_grad.reshape(key_raw.shape),
         v_grad.reshape(value_in.shape),
-        q_gain_grad.reshape(-1),
-        k_gain_grad.reshape(-1),
+        q_gain_grad,
+        k_gain_grad,
     )
 
 

time: 82.3 us -> 77.8 us (0.945)
  local copies, waits for them, and re-layouts: 7.92 us -> 0 us
  Pallas kernels: 71.5 us -> 76.3 us
  other arithmetic: 1.21 us -> 0 us
    unnamed x15 -> x0, local copies, waits for them, and re-layouts: 7.92 us -> none
    pallas_call x0 -> x1, Pallas kernels: none -> 3.18 us  [head_body(): pl.pallas_call(store_kernel, out_shape=(rows, rows, rows, gain_rows, gain...]
    pallas_call x1, Pallas kernels: 71.5 us -> 73.1 us  [head_body(): pl.pallas_call(functools.partial(head_kernel, sizes), out_shape=(rows, ro...]
    pallas_call x2 -> x0, other arithmetic: 1.21 us -> none  [head_body(): pl.pallas_call(functools.partial(head_kernel, sizes), out_shape=(rows, ro...]
where the time goes in v2:
time: 77.8 us; the launch traced here: 77.5 us
  Pallas kernels  76.3 us (98%)
  between operations  1.29 us (2%)
    pallas_call x1, Pallas kernels, head_body(): pl.pallas_call(functools.partial(head_kernel, sizes), out_shape=(rows, ro...  73.1 us
    pallas_call x1, Pallas kernels, head_body(): pl.pallas_call(store_kernel, out_shape=(rows, rows, rows, gain_rows, gain...  3.18 us

profile of v2, /device:TPU:0, one launch (start us, length us, event | category | flops | bytes accessed | tf_op | source)
XLA Modules:
  0.0 77.5 jit_solution(18023026183368914893)
XLA Ops:
  1.3 73.1 %shard_map.110 = (bf16[128,3072]{1,0:T(8,128)(2,1)}, bf16[128,3072]{1,0:T(8,128)(2,1)}, bf16[128,3072]{1,0:T(8,128)(2,1)}, f32[768]{0:T(1024)}, f32[768]{0:T(1024)}) custom-call(s32[1,1]{1,0:T(1,128)S(6)} %copy.12.attend_ref, bf16[128,3072]{1,0:T(8,128)(2,1)} %bitcast.9, bf16[128,3072]{1,0:T(8,128)(2,1)} %bitcast.10, bf16[128,3072]{1,0:T(8,128)(2,1)} %bitcast.11, ...), custom_call_target="tpu_custom_call" | custom-call | tf_op jit(solution)/shard_map/pallas_call | solution.py:357
  74.4 3.2 %shard_map.111 = (bf16[128,3072]{1,0:T(8,128)(2,1)}, bf16[128,3072]{1,0:T(8,128)(2,1)}, bf16[128,3072]{1,0:T(8,128)(2,1)}, f32[768]{0:T(1024)}, f32[768]{0:T(1024)}) custom-call(bf16[128,3072]{1,0:T(8,128)(2,1)} %get-tuple-element.15.refs_0_, bf16[128,3072]{1,0:T(8,128)(2,1)} %get-tuple-element.16.refs_1_, bf16[128,3072]{1,0:T(8,128)(2,1)} %get-tuple-element.17.refs_2_, ...), custom_call_target="tpu_custom_call" | custom-call | tf_op jit(solution)/shard_map/pallas_call | solution.py:395

commit v3 on v2

--- a/solution.py
+++ b/solution.py
@@ -74,9 +74,9 @@
     sizes,
     attend_ref, q_hbm, k_hbm, v_hbm, c_hbm, q_gain, k_gain,
     q_out, k_out, v_out, q_gain_out, k_gain_out,
-    raw, normed, inv, heads, grads, back, first, acc, terms, gathered,
+    raw, normed, inv, heads, grads, back, first, acc, gathered, summed, totals,
     raw_sem, send_sem, recv_sem, back_send, back_recv,
-    first_send, first_recv, terms_send, terms_recv,
+    first_send, first_recv, clip_send, clip_recv, totals_send, totals_recv,
 ):
     groups, seqs, reps, tokens, width, per_owner = sizes
     owners = groups * seqs
@@ -87,31 +87,24 @@
     me = group * seqs + seq
     factor = HEAD_DIM ** (-0.5)
 
+    def partner(step):
+        other = lax.rem(me + step, owners)
+        return other, {"group": other // seqs, "seq": lax.rem(other, seqs)}
+
+    def clip_partner(step):
+        return {"rep": lax.rem(rep + step, reps)}
+
+    places = [partner(step)[1] for step in range(1, owners)]
+    places += [clip_partner(step) for step in range(1, reps)]
+    barrier = pltpu.get_barrier_semaphore()
+    for place in places:
+        pl.semaphore_signal(barrier, inc=1, device_id=place, device_id_type=MESH)
+
     loads = []
     for which, source in enumerate((q_hbm, k_hbm)):
         load = pltpu.make_async_copy(source, raw.at[which], raw_sem.at[which])
         load.start()
         loads.append(load)
-
-    barrier = pltpu.get_barrier_semaphore()
-    devices = owners * reps
-    flat = me * reps + rep
-
-    def greet(step, carry):
-        other = lax.rem(flat + step, devices)
-        place = {
-            "group": other // (seqs * reps),
-            "seq": lax.rem(other // reps, seqs),
-            "rep": lax.rem(other, reps),
-        }
-        pl.semaphore_signal(barrier, inc=1, device_id=place, device_id_type=MESH)
-        return carry
-
-    lax.fori_loop(1, devices, greet, 0)
-
-    def partner(step):
-        other = lax.rem(me + step, owners)
-        return other, {"group": other // seqs, "seq": lax.rem(other, seqs)}
 
     my_rows = pl.ds(pl.multiple_of(me * tokens, tokens), tokens)
 
@@ -145,7 +138,7 @@
         lax.fori_loop(0, tokens // ROWS, step, 0)
 
     first[me] = jnp.full(first.shape[1:], attend_ref[0, 0].astype(jnp.float32))
-    pl.semaphore_wait(barrier, devices - 1)
+    pl.semaphore_wait(barrier, len(places))
     for step in range(1, owners):
         other, place = partner(step)
         pltpu.make_async_remote_copy(
@@ -172,7 +165,7 @@
 
     lax.fori_loop(1, per_owner, send_rest, 0)
 
-    terms[...] = jnp.zeros(terms.shape, jnp.float32)
+    gathered[rep] = jnp.zeros(gathered.shape[1:], jnp.float32)
     few = first.at[pl.ds(0, owners - 1)]
     pltpu.make_async_copy(few, few, first_recv).wait()
 
@@ -236,8 +229,8 @@
             q_terms = q_terms + jnp.sum(
                 q_low.astype(jnp.float32) * q_block.astype(jnp.float32), axis=0, keepdims=True
             )
-        terms[head, 0:1, :] = q_terms / q_gain[:, columns(me, head)]
-        terms[head, 1:2, :] = k_terms / k_gain[:, columns(me, head)]
+        gathered[rep, head, 0:1, :] = q_terms / q_gain[:, columns(me, head)]
+        gathered[rep, head, 1:2, :] = k_terms / k_gain[:, columns(me, head)]
         for which, landing in ((0, back.at[0]), (1, back.at[1]), (2, v_out)):
             for step in range(1, owners):
                 other, place = partner(step)
@@ -256,29 +249,15 @@
 
     lax.fori_loop(0, per_owner, one_head, 0)
 
-    target_rep = me // per_rep
-    slot = rep * per_rep + lax.rem(me, per_rep)
-
-    def send_terms(place):
+    for step in range(1, reps):
         pltpu.make_async_remote_copy(
-            src_ref=terms,
-            dst_ref=gathered.at[slot],
-            send_sem=terms_send,
-            recv_sem=terms_recv,
-            device_id={**place, "rep": target_rep},
+            src_ref=gathered.at[rep],
+            dst_ref=gathered.at[rep],
+            send_sem=clip_send,
+            recv_sem=clip_recv,
+            device_id=clip_partner(step),
             device_id_type=MESH,
         ).start()
-
-    for step in range(1, owners):
-        send_terms(partner(step)[1])
-
-    @pl.when(rep != target_rep)
-    def _():
-        send_terms(partner(0)[1])
-
-    @pl.when(rep == target_rep)
-    def _():
-        pltpu.make_async_copy(terms, gathered.at[slot], terms_recv).start()
 
     def denormalize_rows(which, gain_ref, out_ref):
         def step(index, carry):
@@ -293,17 +272,36 @@
 
         lax.fori_loop(0, tokens // ROWS, step, 0)
 
-    for which, gain_ref, out_ref in ((0, q_gain, q_out), (1, k_gain, k_out)):
-        pltpu.make_async_copy(back.at[which], back.at[which], back_recv.at[which]).wait()
-        denormalize_rows(which, gain_ref, out_ref)
-
-    pltpu.make_async_copy(gathered, gathered, terms_recv).wait()
+    pltpu.make_async_copy(back.at[0], back.at[0], back_recv.at[0]).wait()
+    denormalize_rows(0, q_gain, q_out)
+
+    other_clips = gathered.at[pl.ds(0, reps - 1)]
+    pltpu.make_async_copy(other_clips, other_clips, clip_recv).wait()
+    summed[...] = sum(gathered[clip] for clip in range(reps))
+    slot = lax.rem(me, per_rep)
+
+    @pl.when(me // per_rep == rep)
+    def _():
+        for step in range(1, owners):
+            pltpu.make_async_remote_copy(
+                src_ref=summed,
+                dst_ref=totals.at[slot],
+                send_sem=totals_send,
+                recv_sem=totals_recv,
+                device_id=partner(step)[1],
+                device_id_type=MESH,
+            ).start()
+        pltpu.make_async_copy(summed, totals.at[slot], totals_recv).start()
+
+    pltpu.make_async_copy(back.at[1], back.at[1], back_recv.at[1]).wait()
+    denormalize_rows(1, k_gain, k_out)
+
+    pltpu.make_async_copy(totals, totals, totals_recv).wait()
     for sub in range(per_rep):
         for head in range(per_owner):
             lanes = slice((sub * per_owner + head) * HEAD_DIM, (sub * per_owner + head + 1) * HEAD_DIM)
-            sums = sum(gathered[clip * per_rep + sub, head] for clip in range(reps))
-            q_gain_out[lanes] = sums[0]
-            k_gain_out[lanes] = sums[1]
+            q_gain_out[lanes] = totals[sub, head, 0]
+            k_gain_out[lanes] = totals[sub, head, 1]
     pltpu.make_async_copy(v_out, v_out, back_recv.at[2]).wait()
 
     pltpu.make_async_copy(few, few, first_send).wait()
@@ -314,12 +312,12 @@
     for which in range(3):
         sent = grads.at[which, :, pl.ds(0, (owners - 1) * tokens)]
         pltpu.make_async_copy(sent, sent, back_send.at[which]).wait()
-    sent = gathered.at[pl.ds(0, owners - 1)]
-    pltpu.make_async_copy(sent, sent, terms_send).wait()
-
-    @pl.when(rep != target_rep)
+    pltpu.make_async_copy(other_clips, other_clips, clip_send).wait()
+
+    @pl.when(me // per_rep == rep)
     def _():
-        pltpu.make_async_copy(terms, terms, terms_send).wait()
+        sent = acc.at[0, pl.ds(0, (owners - 1) * per_owner * 8)]
+        pltpu.make_async_copy(sent, sent, totals_send).wait()
 
 
 def store_kernel(*refs):
@@ -368,13 +366,16 @@
             pltpu.VMEM((2, tokens, width), low),
             pltpu.VMEM((owners, 8, group_len), jnp.float32),
             pltpu.VMEM((2, clip_len, HEAD_DIM), jnp.float32),
+            pltpu.VMEM((reps, per_owner, 8, HEAD_DIM), jnp.float32),
             pltpu.VMEM((per_owner, 8, HEAD_DIM), jnp.float32),
-            pltpu.VMEM((owners, per_owner, 8, HEAD_DIM), jnp.float32),
+            pltpu.VMEM((owners // reps, per_owner, 8, HEAD_DIM), jnp.float32),
             dma((2,)),
             dma((4, per_owner)),
             dma((4, per_owner)),
             dma((3,)),
             dma((3,)),
+            dma,
+            dma,
             dma,
             dma,
             dma,
@@ -540,7 +541,7 @@
     owners = lax.axis_size("group") * lax.axis_size("seq")
     heads = width // HEAD_DIM
     even = heads % owners == 0 and owners % lax.axis_size("rep") == 0
-    if even and tokens * owners * heads <= 32768 and tokens % 16 == 0:
+    if even and tokens * owners * heads <= 32768 and tokens % 16 == 0 and tokens * owners >= heads * 8:
         return head_body(*arrays)
     return ring_body(*arrays)
 

time: 77.8 us -> 75.3 us (0.968)
  Pallas kernels: 76.3 us -> 73.7 us
    pallas_call x1, Pallas kernels: 73.1 us -> 70.5 us  [head_body(): pl.pallas_call(functools.partial(head_kernel, sizes), out_shape=(rows, ro...]
where the time goes in v3:
time: 75.3 us; the launch traced here: 75 us
  Pallas kernels  73.7 us (98%)
  between operations  1.29 us (2%)
    pallas_call x1, Pallas kernels, head_body(): pl.pallas_call(functools.partial(head_kernel, sizes), out_shape=(rows, ro...  70.5 us
    pallas_call x1, Pallas kernels, head_body(): pl.pallas_call(store_kernel, out_shape=(rows, rows, rows, gain_rows, gain...  3.18 us

profile of v3, /device:TPU:0, one launch (start us, length us, event | category | flops | bytes accessed | tf_op | source)
XLA Modules:
  0.0 75.0 jit_solution(3803034917174538623)
XLA Ops:
  1.3 70.5 %shard_map.110 = (bf16[128,3072]{1,0:T(8,128)(2,1)}, bf16[128,3072]{1,0:T(8,128)(2,1)}, bf16[128,3072]{1,0:T(8,128)(2,1)}, f32[768]{0:T(1024)}, f32[768]{0:T(1024)}) custom-call(s32[1,1]{1,0:T(1,128)S(6)} %copy.12.attend_ref, bf16[128,3072]{1,0:T(8,128)(2,1)} %bitcast.9, bf16[128,3072]{1,0:T(8,128)(2,1)} %bitcast.10, bf16[128,3072]{1,0:T(8,128)(2,1)} %bitcast.11, ...), custom_call_target="tpu_custom_call" | custom-call | tf_op jit(solution)/shard_map/pallas_call | solution.py:355
  71.8 3.2 %shard_map.111 = (bf16[128,3072]{1,0:T(8,128)(2,1)}, bf16[128,3072]{1,0:T(8,128)(2,1)}, bf16[128,3072]{1,0:T(8,128)(2,1)}, f32[768]{0:T(1024)}, f32[768]{0:T(1024)}) custom-call(bf16[128,3072]{1,0:T(8,128)(2,1)} %get-tuple-element.15.refs_0_, bf16[128,3072]{1,0:T(8,128)(2,1)} %get-tuple-element.16.refs_1_, bf16[128,3072]{1,0:T(8,128)(2,1)} %get-tuple-element.17.refs_2_, ...), custom_call_target="tpu_custom_call" | custom-call | tf_op jit(solution)/shard_map/pallas_call | solution.py:396

commit v4 on v3

--- a/solution.py
+++ b/solution.py
@@ -85,16 +85,17 @@
     per_rep = owners // reps
     group, seq, rep = lax.axis_index("group"), lax.axis_index("seq"), lax.axis_index("rep")
     me = group * seqs + seq
+    order = sorted(range(1, owners), key=lambda step: step == seqs)
     factor = HEAD_DIM ** (-0.5)
 
     def partner(step):
-        other = lax.rem(me + step, owners)
+        other = jnp.bitwise_xor(me, step)
         return other, {"group": other // seqs, "seq": lax.rem(other, seqs)}
 
     def clip_partner(step):
         return {"rep": lax.rem(rep + step, reps)}
 
-    places = [partner(step)[1] for step in range(1, owners)]
+    places = [partner(step)[1] for step in order]
     places += [clip_partner(step) for step in range(1, reps)]
     barrier = pltpu.get_barrier_semaphore()
     for place in places:
@@ -112,7 +113,7 @@
         return pl.ds(pl.multiple_of(owner * own_width + head * HEAD_DIM, HEAD_DIM), HEAD_DIM)
 
     def send_heads(which, source, head):
-        for step in range(1, owners):
+        for step in order:
             other, place = partner(step)
             pltpu.make_async_remote_copy(
                 src_ref=source.at[:, columns(other, head)],
@@ -139,7 +140,7 @@
 
     first[me] = jnp.full(first.shape[1:], attend_ref[0, 0].astype(jnp.float32))
     pl.semaphore_wait(barrier, len(places))
-    for step in range(1, owners):
+    for step in order:
         other, place = partner(step)
         pltpu.make_async_remote_copy(
             src_ref=first.at[me],
@@ -232,7 +233,7 @@
         gathered[rep, head, 0:1, :] = q_terms / q_gain[:, columns(me, head)]
         gathered[rep, head, 1:2, :] = k_terms / k_gain[:, columns(me, head)]
         for which, landing in ((0, back.at[0]), (1, back.at[1]), (2, v_out)):
-            for step in range(1, owners):
+            for step in order:
                 other, place = partner(step)
                 pltpu.make_async_remote_copy(
                     src_ref=grads.at[which, head, pl.ds(pl.multiple_of(other * tokens, tokens), tokens)],
@@ -282,7 +283,7 @@
 
     @pl.when(me // per_rep == rep)
     def _():
-        for step in range(1, owners):
+        for step in order:
             pltpu.make_async_remote_copy(
                 src_ref=summed,
                 dst_ref=totals.at[slot],
@@ -540,7 +541,7 @@
     tokens, width = arrays[0].shape[2:]
     owners = lax.axis_size("group") * lax.axis_size("seq")
     heads = width // HEAD_DIM
-    even = heads % owners == 0 and owners % lax.axis_size("rep") == 0
+    even = heads % owners == 0 and owners & (owners - 1) == 0 and owners % lax.axis_size("rep") == 0
     if even and tokens * owners * heads <= 32768 and tokens % 16 == 0 and tokens * owners >= heads * 8:
         return head_body(*arrays)
     return ring_body(*arrays)

time: 75.3 us -> 74.5 us (0.989)
  Pallas kernels: 73.7 us -> 72.9 us
    pallas_call x1, Pallas kernels: 70.5 us -> 69.8 us  [head_body(): pl.pallas_call(functools.partial(head_kernel, sizes), out_shape=(rows, ro...]
where the time goes in v4:
time: 74.5 us; the launch traced here: 74.2 us
  Pallas kernels  72.9 us (98%)
  between operations  1.29 us (2%)
    pallas_call x1, Pallas kernels, head_body(): pl.pallas_call(functools.partial(head_kernel, sizes), out_shape=(rows, ro...  69.8 us
    pallas_call x1, Pallas kernels, head_body(): pl.pallas_call(store_kernel, out_shape=(rows, rows, rows, gain_rows, gain...  3.18 us

profile of v4, /device:TPU:0, one launch (start us, length us, event | category | flops | bytes accessed | tf_op | source)
XLA Modules:
  0.0 74.2 jit_solution(509216363476865338)
XLA Ops:
  1.3 69.8 %shard_map.110 = (bf16[128,3072]{1,0:T(8,128)(2,1)}, bf16[128,3072]{1,0:T(8,128)(2,1)}, bf16[128,3072]{1,0:T(8,128)(2,1)}, f32[768]{0:T(1024)}, f32[768]{0:T(1024)}) custom-call(s32[1,1]{1,0:T(1,128)S(6)} %copy.12.attend_ref, bf16[128,3072]{1,0:T(8,128)(2,1)} %bitcast.9, bf16[128,3072]{1,0:T(8,128)(2,1)} %bitcast.10, bf16[128,3072]{1,0:T(8,128)(2,1)} %bitcast.11, ...), custom_call_target="tpu_custom_call" | custom-call | tf_op jit(solution)/shard_map/pallas_call | solution.py:356
  71.1 3.2 %shard_map.111 = (bf16[128,3072]{1,0:T(8,128)(2,1)}, bf16[128,3072]{1,0:T(8,128)(2,1)}, bf16[128,3072]{1,0:T(8,128)(2,1)}, f32[768]{0:T(1024)}, f32[768]{0:T(1024)}) custom-call(bf16[128,3072]{1,0:T(8,128)(2,1)} %get-tuple-element.15.refs_0_, bf16[128,3072]{1,0:T(8,128)(2,1)} %get-tuple-element.16.refs_1_, bf16[128,3072]{1,0:T(8,128)(2,1)} %get-tuple-element.17.refs_2_, ...), custom_call_target="tpu_custom_call" | custom-call | tf_op jit(solution)/shard_map/pallas_call | solution.py:397
